TPU v7x, 128 devices: a whole 4x4x4 slice. The times are simulated.
128 devices in a mesh: node: 4 (over z_lo, core), dp: 32 (over z_hi, x, y).
Axes of the slice: x: 4, y: 4, z: 4 (z_hi: 2, z_lo: 2; z = z_hi * 2 + z_lo), core: 2. Of those that a mesh axis runs over, the one named last changes fastest.
Arguments:
- tokens: bfloat16 [65536, 4096], P(('node', 'dp')), may hold values from -24 to 24
- cotangent: bfloat16 [65536, 1792], P(('node', 'dp')), may hold values from -6 to 6
- master: float32 [1792, 4096], P('node', 'dp'), may hold values from -3 to 3
- moment_one: float32 [1792, 4096], P('node', 'dp'), may hold values from -6 to 6
- moment_two: float32 [1792, 4096], P('node', 'dp'), may hold values from 0.25 to 4
Outputs:
- outputs: bfloat16 [65536, 1792], P(('node', 'dp'))
- input_grad: bfloat16 [65536, 4096], P(('node', 'dp'))
- new_master: float32 [1792, 4096], P('node', 'dp')
- new_one: float32 [1792, 4096], P('node', 'dp')
- new_two: float32 [1792, 4096], P('node', 'dp')
- new_copy: bfloat16 [1792, 4096], P('node')
All inputs are finite; a program needn't handle non-finite values.
Results may differ from a plain program's by a relative error of at most 0.005.
Values may be sent and summed in bfloat16 or wider, within the bound.
A program may use at most 128 MiB of HBM per device.

v0:
```python
import math

import jax
import jax.numpy as jnp
from jax import lax
from jax.sharding import PartitionSpec as P

beta_one = 0.9
beta_two = 0.95
epsilon = 1e-08
step_size = 0.2
decay_rate = 0.1
step_count = 10


def spread_copy(weights):
    return lax.all_gather(weights.astype(jnp.bfloat16), "dp", axis=1, tiled=True)


def against_rows(left, right):
    return lax.dot_general(
        left, right, (((1,), (1,)), ((), ())), preferred_element_type=jnp.float32
    )


def local(tokens, cotangent, master, moment_one, moment_two):
    rows_here = tokens.shape[0]
    width = tokens.shape[1]
    hidden = cotangent.shape[1]
    local_copy = spread_copy(master)
    weights = lax.all_gather(local_copy, "node", axis=0, tiled=True)
    forward = against_rows(tokens, weights)
    backward = jnp.dot(cotangent, weights, preferred_element_type=jnp.float32)
    outputs = (forward / math.sqrt(width)).astype(jnp.bfloat16)
    input_grad = (backward / math.sqrt(hidden)).astype(jnp.bfloat16)
    group_sum = lax.psum_scatter(
        lax.dot_general(
            cotangent, tokens, (((0,), (0,)), ((), ())), preferred_element_type=jnp.float32
        ).astype(jnp.bfloat16),
        "node",
        scatter_dimension=0,
        tiled=True,
    )
    weight_sum = lax.psum_scatter(group_sum, "dp", scatter_dimension=1, tiled=True).astype(
        jnp.float32
    )
    total_tokens = rows_here * lax.axis_size("node") * lax.axis_size("dp")
    grad = weight_sum / math.sqrt(total_tokens)
    new_one = beta_one * moment_one + (1.0 - beta_one) * grad
    new_two = beta_two * moment_two + (1.0 - beta_two) * grad * grad
    first_fix = 1.0 - beta_one**step_count
    second_fix = 1.0 - beta_two**step_count
    update = new_one / first_fix / (jnp.sqrt(new_two / second_fix) + epsilon)
    new_master = master - step_size * (update + decay_rate * master)
    new_copy = spread_copy(new_master)
    return (outputs, input_grad, new_master, new_one, new_two, new_copy)


def solution(mesh):
    placed = (
        P(("node", "dp"), None),
        P(("node", "dp"), None),
        P("node", "dp"),
        P("node", "dp"),
        P("node", "dp"),
    )
    return jax.shard_map(
        local,
        mesh=mesh,
        in_specs=placed,
        out_specs=(
            P(("node", "dp"), None),
            P(("node", "dp"), None),
            P("node", "dp"),
            P("node", "dp"),
            P("node", "dp"),
            P("node", None),
        ),
        check_vma=False,
    )
```

profile of v0, /device:TPU:0, one launch (start us, length us, event | category | flops | bytes accessed | tf_op | source)
XLA Modules:
  0.0 707.0 jit_solution(11173175080292778607)
XLA Ops:
  7.2 0.0 copy-start
  7.2 0.0 reduce-scatter.5.cloned.1.call-start
  7.2 1.4 copy-done
  8.7 13.3 %convolution_convert_fusion = bf16[1792,4096]{1,0:T(8,128)(2,1)} fusion(bf16[512,1792]{1,0:T(8,128)(2,1)S(1)} %copy-done, bf16[512,4096]{1,0:T(8,128)(2,1)} %param.5), kind=kOutput, calls=%fused_computation | convolution fusion | flops 7523532800 | bytes 20709376 | tf_op jit(solution)/shard_map/dot_general | solution.py:37
  21.9 0.0 reduce-scatter.5.cloned.1.call-update
  22.0 0.0 copy-start.2
  22.0 0.0 copy-start.3
  22.0 0.0 copy-start.4
  22.0 0.0 reduce-scatter.7.cloned.1.call-start
  22.1 132.6 %reduce-scatter.5.cloned.1.call-done = bf16[448,4096]{1,0:T(8,128)(2,1)} async-done(((bf16[1792,4096]{1,0:T(8,128)(2,1)}), bf16[448,4096]{1,0:T(8,128)(2,1)}) %reduce-scatter.5.cloned.1.call-update) | async-done | bytes 3670032 | tf_op jit(solution)/shard_map/reduce_scatter | solution.py:36
  154.7 6.3 copy.11
  161.0 0.0 reduce-scatter.7.cloned.1.call-update
  161.0 0.0 all-gather.4.cloned.1.call-start
  161.1 193.4 %reduce-scatter.7.cloned.1.call-done = bf16[128,448]{1,0:T(8,128)(2,1)} async-done(((bf16[4096,448]{1,0:T(8,128)(2,1)}), bf16[128,448]{1,0:T(8,128)(2,1)}) %reduce-scatter.7.cloned.1.call-update) | async-done | bytes 114704
  354.5 1.0 copy.12
  355.5 0.0 copy-done.2
  355.5 0.0 copy-done.3
  355.6 0.0 copy-done.4
  355.6 1.0 fusion.3
  356.6 0.0 all-gather.4.cloned.1.call-update
  356.6 0.0 all-gather.8.cloned.1.call-start
  356.7 0.5 all-gather.8.cloned.1.call-update
  357.2 0.0 all-gather.6.cloned.1.call-start
  357.3 88.4 %all-gather.4.cloned.1.call-done = bf16[448,4096]{1,0:T(8,128)(2,1)} async-done(((bf16[448,128]{1,0:T(8,128)(2,1)}), bf16[448,4096]{1,0:T(8,128)(2,1)}) %all-gather.4.cloned.1.call-update) | async-done | bytes 3670032 | tf_op jit(solution)/shard_map/all_gather | solution.py:17
  445.6 0.0 all-gather.6.cloned.1.call-update
  445.7 94.9 %all-gather.8.cloned.1.call-done = bf16[448,4096]{1,0:T(8,128)(2,1)} async-done(((bf16[448,128]{1,0:T(8,128)(2,1)}), bf16[448,4096]{1,0:T(8,128)(2,1)}) %all-gather.8.cloned.1.call-update) | async-done | bytes 3670032 | tf_op jit(solution)/shard_map/all_gather | solution.py:17
  540.6 131.9 %all-gather.6.cloned.1.call-done = bf16[1792,4096]{1,0:T(8,128)(2,1)} async-done(((bf16[448,4096]{1,0:T(8,128)(2,1)}), bf16[1792,4096]{1,0:T(8,128)(2,1)}) %all-gather.6.cloned.1.call-update) | async-done | bytes 14680080 | tf_op jit(solution)/shard_map/all_gather | solution.py:31
  672.5 0.0 copy-start.5
  672.5 12.5 %multiply_convert_fusion = bf16[512,4096]{1,0:T(8,128)(2,1)} fusion(bf16[512,1792]{1,0:T(8,128)(2,1)S(1)} %copy-done, bf16[1792,4096]{1,0:T(8,128)(2,1)} %all-gather.6.cloned.1.call-done), kind=kOutput, calls=%fused_computation.1 | convolution fusion | flops 7520387072 | bytes 20709376 | tf_op jit(solution)/shard_map/dot_general | solution.py:33
  685.0 0.0 copy-done.5
  685.0 0.0 copy-start.1
  685.0 13.6 %multiply_convert_fusion.1 = bf16[512,1792]{1,0:T(8,128)(2,1)} fusion(bf16[512,4096]{1,0:T(8,128)(2,1)S(1)} %copy-done.5, bf16[1792,4096]{1,0:T(8,128)(2,1)} %all-gather.6.cloned.1.call-done), kind=kOutput, calls=%fused_computation.2 | convolution fusion | flops 7518027776 | bytes 20709376 | tf_op jit(solution)/shard_map/dot_general | solution.py:21
  698.7 0.0 copy-done.1
  698.7 1.8 copy.14
Async XLA Ops:
  7.2 1.5 copy-start
  7.2 147.5 %reduce-scatter.5.cloned.1.call-start = ((), (), s32[]{:S(2)}) async-start(), calls=%async_computation.4 | async-start | bytes 18350080 | tf_op jit(solution)/shard_map/reduce_scatter | solution.py:36
  22.0 333.6 %copy-start.2 = (f32[448,128]{1,0:T(8,128)S(1)}, f32[448,128]{1,0:T(8,128)}, u32[]{:S(2)}) copy-start(f32[448,128]{1,0:T(8,128)} %param.7) | copy-start | bytes 688132
  22.0 333.6 %copy-start.3 = (f32[448,128]{1,0:T(8,128)S(1)}, f32[448,128]{1,0:T(8,128)}, u32[]{:S(2)}) copy-start(f32[448,128]{1,0:T(8,128)} %param.8) | copy-start | bytes 688132
  22.0 333.6 %copy-start.4 = (f32[448,128]{1,0:T(8,128)S(1)}, f32[448,128]{1,0:T(8,128)}, u32[]{:S(2)}) copy-start(f32[448,128]{1,0:T(8,128)} %param.9) | copy-start | bytes 688132
  22.0 332.5 %reduce-scatter.7.cloned.1.call-start = ((), (), s32[]{:S(2)}) async-start(), calls=%async_computation.6 | async-start | bytes 4325376
  161.0 284.6 %all-gather.4.cloned.1.call-start = ((), (), s32[]{:S(2)}) async-start(), calls=%async_computation.2 | async-start | bytes 3784704 | tf_op jit(solution)/shard_map/all_gather | solution.py:17
  356.6 184.0 %all-gather.8.cloned.1.call-start = ((), (), s32[]{:S(2)}) async-start(), calls=%async_computation.5 | async-start | bytes 3784704 | tf_op jit(solution)/shard_map/all_gather | solution.py:17
  357.2 315.3 %all-gather.6.cloned.1.call-start = ((), (), s32[]{:S(2)}) async-start(), calls=%async_computation.3 | async-start | bytes 18350080 | tf_op jit(solution)/shard_map/all_gather | solution.py:31
  672.5 12.5 %copy-start.5 = (bf16[512,4096]{1,0:T(8,128)(2,1)S(1)}, bf16[512,4096]{1,0:T(8,128)(2,1)}, u32[]{:S(2)}) copy-start(bf16[512,4096]{1,0:T(8,128)(2,1)} %param.5) | copy-start | bytes 12582916
  685.0 13.7 %copy-start.1 = (bf16[448,4096]{1,0:T(8,128)(2,1)S(1)}, bf16[448,4096]{1,0:T(8,128)(2,1)}, u32[]{:S(2)}) copy-start(bf16[448,4096]{1,0:T(8,128)(2,1)} %all-gather.8.cloned.1.call-done) | copy-start | bytes 11010052
Sparse Core Ops, SparseCore 0:
  22.1 132.5 reduce-scatter.4
  161.2 193.2 reduce-scatter.6
  357.8 87.7 all-gather.3
  448.8 91.7 all-gather.7
  542.1 130.3 all-gather.5
where the time goes:
time: 711 us; the launch traced here: 707 us
  waiting for transfers between devices  642 us (90%)
  matrix products  39.4 us (6%)
  between operations  13.8 us (2%)
  local copies, waits for them, and re-layouts  10.7 us (2%)
    unnamed x6, waiting for transfers between devices  194 us
    all_gather x2, waiting for transfers between devices, spread_copy(): lax.all_gather(weights.astype(jnp.bfloat16), 'dp', axis=1, tiled=True)  183 us
    reduce_scatter x1, waiting for transfers between devices, local(): lax.psum_scatter(lax.dot_general(cotangent, tokens, (((0,), (0,)), ((), (...  133 us
    all_gather x1, waiting for transfers between devices, local(): weights = lax.all_gather(local_copy, 'node', axis=0, tiled=True)  132 us
  transfers between devices with their start and end apart: 5, of which 5 were waited for; matrix products, arithmetic and copies ran while one was open for 0% of the time, Pallas kernels for 0%

commit v1 on v0

v1 whole, which is shorter than its diff:
```python
import math

import jax
import jax.numpy as jnp
from jax import lax
from jax.experimental import pallas as pl
from jax.experimental.pallas import tpu as pltpu
from jax.sharding import PartitionSpec as P

beta_one = 0.9
beta_two = 0.95
epsilon = 1e-08
step_size = 0.2
decay_rate = 0.1
step_count = 10

MESH = pl.DeviceIdType.MESH
AXES = ("z", "x", "y")
BF = jnp.bfloat16
F32 = jnp.float32

ROWS = 448
PAD = 512
LANE = 128
TOK = 512
CHUNK = 512
N_CHUNK = 8
PARTS = ((0, 192, "xyz"), (192, 128, "yzx"), (320, 128, "zxy"))
COPY_PARTS = ((0, 224, "xy"), (224, 224, "yx"))


def device_at(co):
    return (
        lax.rem(co["z"], 2) * 2 + co["c"],
        lax.div(co["z"], 2) * 16 + co["x"] * 4 + co["y"],
    )


def moved(co, axis, by):
    other = dict(co)
    other[axis] = lax.rem(co[axis] + by + 4, 4)
    return other


def kernel(
    tokens, cotangent, master, moment_one, moment_two,
    outputs, input_grad, new_master, new_one, new_two, copies,
    tok, cot, cot_t, weights, terms,
    got1a, got1b, got1c, got2a, got2b, got2c, got3a, got3b, got3c,
    grad_sum, out_acc, ig_own, ig_send, ig_recv, out_send, out_recv, out_full,
    state, state_new, copy_own,
    load_sem, tok_sem, ig_out_sem,
    core_send, core_recv, ag_send, ag_recv, rs_send, rs_recv, nc_send, nc_recv,
):
    node = lax.axis_index("node")
    dp = lax.axis_index("dp")
    c = lax.rem(node, 2)
    z_lo = lax.div(node, 2)
    z_hi = lax.div(dp, 16)
    me = {
        "z": z_hi * 2 + z_lo,
        "x": lax.rem(lax.div(dp, 4), 4),
        "y": lax.rem(dp, 4),
        "c": c,
    }
    sibling = device_at({**me, "c": 1 - c})
    opposite_z = device_at(moved(me, "z", 2))
    window = [pl.multiple_of(lo * 896 + c * 384, 128) for lo in range(2)]
    sib_window = [pl.multiple_of(lo * 896 + (1 - c) * 384, 128) for lo in range(2)]
    offset = c * 64

    def remote(src, dst, send, recv, to):
        return pltpu.make_async_remote_copy(
            src_ref=src, dst_ref=dst, send_sem=send, recv_sem=recv,
            device_id=to, device_id_type=MESH,
        )

    def push(src, dst, send, recv, to):
        remote(src, dst, send, recv, to).start()

    def left(src, send, recv):
        remote(src, src, send, recv, sibling).wait_send()

    def arrive(dst, send, recv):
        remote(dst, dst, send, recv, sibling).wait_recv()

    def load_state(k):
        return pltpu.make_async_copy(
            (master, moment_one, moment_two)[k], state.at[k], load_sem.at[k]
        )

    def load_cot(lo):
        return pltpu.make_async_copy(
            cotangent.at[:, pl.ds(window[lo], PAD)],
            cot.at[lo, pl.ds(0, TOK)],
            load_sem.at[3 + lo],
        )

    def chunk_of(i):
        hi = lax.rem(z_hi + 1 - lax.div(i, 4) + 2, 2)
        return hi, lax.rem(me["x"] + 2 + i, 4)

    def columns(q):
        return pl.ds(pl.multiple_of(q * CHUNK, CHUNK), CHUNK)

    def load_tok(i):
        hi, x = chunk_of(i)
        q = hi * 4 + x
        return pltpu.make_async_copy(
            tokens.at[:, columns(q)], tok.at[q, pl.ds(0, TOK)], tok_sem.at[i]
        )

    load_state(0).start()
    load_cot(0).start()
    load_cot(1).start()
    for i in range(N_CHUNK):
        load_tok(i).start()
    load_state(1).start()
    load_state(2).start()

    barrier = pltpu.get_barrier_semaphore()
    peers = [sibling, opposite_z]
    for axis in AXES:
        peers += [device_at(moved(me, axis, 1)), device_at(moved(me, axis, -1))]
    for peer in peers:
        pl.semaphore_signal(barrier, inc=1, device_id=peer, device_id_type=MESH)
    pl.semaphore_wait(barrier, len(peers))

    def rows_of(buffer, first, count):
        if buffer is weights:
            return pl.ds(pl.multiple_of(offset + first, 32), count)
        return pl.ds(first, count)

    class Gather:
        def __init__(self, buffer, names, axis, full, half_axis, first, count, send, recv, base):
            self.buffer, self.names, self.axis, self.full = buffer, names, axis, full
            self.half_axis, self.first, self.count = half_axis, first, count
            self.send, self.recv, self.base = send, recv, base

        def at(self, where, half):
            index = []
            first, count = self.first, self.count
            if self.half_axis is None:
                count = count // 2
                first = first + half * count
            for name in self.names:
                if name == self.half_axis:
                    index.append(pl.ds(half * self.size(name) // 2, self.size(name) // 2))
                elif name == self.axis:
                    index.append(lax.rem(me[name] + where + 4, 4))
                elif name in self.full:
                    index.append(slice(None))
                else:
                    index.append(me[name])
            return self.buffer.at[tuple(index) + (rows_of(self.buffer, first, count), slice(None))]

        def size(self, name):
            return 2 if name == "h" else 4

        def sems(self, way, message):
            k = self.base + way * 3 + message
            return self.send.at[k], self.recv.at[k]

        def start(self):
            for message in range(2):
                for way in range(2):
                    half = message if way == 0 else 1 - message
                    ref = self.at(0, half)
                    push(ref, ref, *self.sems(way, message), device_at(moved(me, self.axis, 1 - 2 * way)))

        def forward(self):
            for way in range(2):
                half = way
                ref = self.at(2 * way - 1, half)
                arrive(ref, *self.sems(way, 0))
                push(ref, ref, *self.sems(way, 2), device_at(moved(me, self.axis, 1 - 2 * way)))

        def finish(self):
            for way in range(2):
                arrive(self.at(2 * way - 1, 1 - way), *self.sems(way, 1))
                arrive(self.at(2, way), *self.sems(way, 2))

        def close(self):
            for way in range(2):
                for message in range(3):
                    left(self.at(0, 0), *self.sems(way, message))

    ag = []
    for p, (first, count, order) in enumerate(PARTS):
        ag.append([
            Gather(
                weights, AXES, order[k], order[:k], order[0] if k else None, first, count,
                ag_send, ag_recv, (p * 3 + k) * 6,
            )
            for k in range(3)
        ])

    nc = []
    for p, (first, count, order) in enumerate(COPY_PARTS):
        nc.append([
            Gather(
                copies, ("h", "x", "y"), order[k], order[:k], "h", first, count,
                nc_send, nc_recv, 2 + (p * 2 + k) * 6,
            )
            for k in range(2)
        ])

    class Reduce:
        def __init__(self, order, stage, first, count, got, base):
            self.order, self.stage, self.first, self.count = order, stage, first, count
            self.axis = order[stage]
            self.got, self.base = got, base

        def index(self, where, half, j=None):
            first, count = self.first, self.count
            if self.stage == 2:
                count = count // 2
                first = first + half * count
            out = []
            for name in AXES:
                k = self.order.index(name)
                if k < self.stage:
                    out.append(me[name])
                elif k == self.stage:
                    out.append(lax.rem(me[name] + where + 4, 4))
                elif k == 2:
                    out.append(pl.ds(2 * half, 2) if j is None else 2 * half + lax.rem(j, 2))
                else:
                    out.append(slice(None) if j is None else lax.div(j, 2))
            return tuple(out) + (pl.ds(first, count), slice(None))

        def got_index(self, slot, j):
            if self.stage == 0:
                names = [n for n in AXES if n != self.axis]
                return (slot,) + tuple(
                    lax.rem(j, 2) if self.order.index(n) == 2 else lax.div(j, 2) for n in names
                )
            if self.stage == 1:
                return (slot, j)
            return (slot,)

        def blocks(self):
            return (8, 2, 1)[self.stage]

        def sems(self, slot):
            return rs_send.at[self.base + slot], rs_recv.at[self.base + slot]

        def out(self, where, half, slot, way):
            push(
                terms.at[self.index(where, half)], self.got.at[slot], *self.sems(slot),
                device_at(moved(me, self.axis, 1 - 2 * way)),
            )

        def start_far(self):
            self.out(2, 0, 0, 0)
            self.out(2, 1, 1, 1)

        def start_near(self, way):
            if way == 0:
                self.out(1, 1, 3, 0)
            else:
                self.out(-1, 0, 5, 1)

        def combine(self):
            for way in range(2):
                arrive(self.got.at[way], *self.sems(way))
                where = 1 - 2 * way

                def add(j, _, way=way, where=where):
                    at = self.index(where, way, j)
                    total = terms[at].astype(F32) + self.got[self.got_index(way, j)].astype(F32)
                    terms[at] = total.astype(BF)
                    return 0

                lax.fori_loop(0, self.blocks(), add, 0)
                self.out(where, way, 2 if way == 0 else 4, way)

        def finish(self):
            for slot in range(2, 6):
                arrive(self.got.at[slot], *self.sems(slot))
            for half, (one, two) in enumerate(((2, 5), (3, 4))):

                def add(j, _, half=half, one=one, two=two):
                    at = self.index(0, half, j)
                    total = (
                        terms[at].astype(F32)
                        + self.got[self.got_index(one, j)].astype(F32)
                        + self.got[self.got_index(two, j)].astype(F32)
                    )
                    if self.stage == 2:
                        size = self.count // 2
                        grad_sum[pl.ds(self.first + half * size, size), :] = total
                    else:
                        terms[at] = total.astype(BF)
                    return 0

                lax.fori_loop(0, self.blocks(), add, 0)

        def close(self):
            for slot in range(6):
                left(self.got.at[slot], *self.sems(slot))

    got = ((got1a, got2a, got3a), (got1b, got2b, got3b), (got1c, got2c, got3c))
    rs = [
        [
            Reduce(order[::-1], k, first, count, got[p][k], (p * 3 + k) * 6)
            for k in range(3)
        ]
        for p, (first, count, order) in enumerate(PARTS)
    ]

    load_state(0).wait()
    weights[me["z"], me["x"], me["y"], pl.ds(pl.multiple_of(offset, 32), ROWS), :] = state[0].astype(BF)
    for p in range(3):
        ag[p][0].start()

    for lo in range(2):
        push(
            cotangent.at[:, pl.ds(sib_window[lo], PAD)], cot.at[lo, pl.ds(TOK, TOK)],
            core_send.at[lo], core_recv.at[lo], sibling,
        )
    for i in range(N_CHUNK):
        hi, x = chunk_of(i)
        q = hi * 4 + x
        push(
            tokens.at[:, columns(q)], tok.at[q, pl.ds(TOK, TOK)],
            core_send.at[2 + i], core_recv.at[2 + i], sibling,
        )

    spare = pl.multiple_of((1 - c) * ROWS, 64)

    def clear(j, _):
        at = (lax.div(j, 16), lax.rem(lax.div(j, 4), 4), lax.rem(j, 4), pl.ds(spare, PAD - ROWS), slice(None))
        weights[at] = jnp.zeros((PAD - ROWS, LANE), BF)
        return 0

    lax.fori_loop(0, 64, clear, 0)

    for lo in range(2):
        load_cot(lo).wait()
        cot_t[lo, :, pl.ds(0, TOK)] = cot[lo, pl.ds(0, TOK), :].T
    for p in range(3):
        ag[p][0].forward()
    for lo in range(2):
        arrive(cot.at[lo, pl.ds(TOK, TOK)], core_send.at[lo], core_recv.at[lo])
        cot_t[lo, :, pl.ds(TOK, TOK)] = cot[lo, pl.ds(TOK, TOK), :].T

    def after(i, step, action):
        pl.when(i == step)(action)

    def each(method, *stages):
        def run():
            for ring in stages:
                getattr(ring, method)()
        return run

    def next_gather(k):
        def run():
            for p in range(3):
                ag[p][k].finish()
                ag[p][k + 1].start()
        return run

    def pass_on(k):
        def run():
            for p in range(3):
                ag[p][k].forward()
        return run

    def term(i, _):
        hi, x = chunk_of(i)
        q = hi * 4 + x
        load_tok(i).wait()
        arrive(tok.at[q, pl.ds(TOK, TOK)], core_send.at[2 + i], core_recv.at[2 + i])
        for lo in range(2):
            part = jnp.dot(
                cot_t[lo, pl.ds(pl.multiple_of(offset, 64), ROWS), :], tok[q],
                preferred_element_type=F32,
            ).astype(BF)
            for y in range(4):
                terms[hi * 2 + lo, x, y] = part[:, y * LANE:(y + 1) * LANE]
        after(i, 0, next_gather(0))
        after(i, 1, pass_on(1))
        after(i, 3, next_gather(1))
        after(i, 3, rs[0][0].start_far)
        after(i, 4, rs[1][0].start_far)
        return 0

    lax.fori_loop(0, N_CHUNK, term, 0)
    rs[2][0].start_far()
    for way in range(2):
        for p in range(3):
            rs[p][0].start_near(way)

    pass_on(2)()
    for p in range(3):
        rs[p][0].combine()
    for p in range(3):
        ag[p][2].finish()

    def next_reduce(k):
        def run():
            for p in range(3):
                rs[p][k].finish()
                rs[p][k + 1].start_far()
                for way in range(2):
                    rs[p][k + 1].start_near(way)
        return run

    def combine(k):
        def run():
            for p in range(3):
                rs[p][k].combine()
        return run

    def update():
        for p in range(3):
            rs[p][2].finish()
        load_state(1).wait()
        load_state(2).wait()
        grad = grad_sum[...] / math.sqrt(TOK * 128)
        one = beta_one * state[1] + (1.0 - beta_one) * grad
        two = beta_two * state[2] + (1.0 - beta_two) * grad * grad
        first_fix = 1.0 - beta_one**step_count
        second_fix = 1.0 - beta_two**step_count
        step = one / first_fix / (jnp.sqrt(two / second_fix) + epsilon)
        moved_master = state[0] - step_size * (step + decay_rate * state[0])
        state_new[0] = moved_master
        state_new[1] = one
        state_new[2] = two
        copy_own[...] = moved_master.astype(BF)
        for k in range(3):
            store_state(k).start()
        store = store_copy()
        store.start()
        for p, (first, count, _) in enumerate(COPY_PARTS):
            push(
                copy_own.at[pl.ds(first, count)],
                copies.at[z_hi, me["x"], me["y"], pl.ds(first, count)],
                nc_send.at[p], nc_recv.at[p], opposite_z,
            )
        store.wait()

    def store_state(k):
        return pltpu.make_async_copy(
            state_new.at[k], (new_master, new_one, new_two)[k], load_sem.at[5 + k]
        )

    def store_copy():
        return pltpu.make_async_copy(
            copy_own, copies.at[z_hi, me["x"], me["y"]], load_sem.at[8]
        )

    def copy_start():
        for p, (first, count, _) in enumerate(COPY_PARTS):
            arrive(
                copies.at[1 - z_hi, me["x"], me["y"], pl.ds(first, count)],
                nc_send.at[p], nc_recv.at[p],
            )
        for p in range(2):
            nc[p][0].start()

    def copy_forward(k):
        def run():
            for p in range(2):
                nc[p][k].forward()
        return run

    def copy_next():
        for p in range(2):
            nc[p][0].finish()
            nc[p][1].start()

    inv_width = 1.0 / math.sqrt(4096)
    inv_hidden = 1.0 / math.sqrt(1792)

    def ig_chunk(i):
        hi, x = chunk_of(i)
        return hi * 4 + x

    def store_ig(i):
        return pltpu.make_async_copy(
            ig_recv.at[i], input_grad.at[:, columns(ig_chunk(i))], ig_out_sem.at[i]
        )

    def close_ig(i):
        arrive(ig_recv.at[i], core_send.at[10 + i], core_recv.at[10 + i])
        total = ig_own[lax.rem(i, 2)] + ig_recv[i].astype(F32)
        ig_recv[i] = (total * inv_hidden).astype(BF)
        store_ig(i).start()

    def against(i, _):
        hi, x = chunk_of(i)
        q = hi * 4 + x
        block = [
            jnp.concatenate([weights[hi * 2 + lo, x, y] for y in range(4)], axis=1)
            for lo in range(2)
        ]

        def backward(first):
            return sum(
                jnp.dot(cot[lo, pl.ds(first, TOK), :], block[lo], preferred_element_type=F32)
                for lo in range(2)
            )

        ig_send[i] = backward(TOK).astype(BF)
        push(ig_send.at[i], ig_recv.at[i], core_send.at[10 + i], core_recv.at[10 + i], sibling)
        ig_own[lax.rem(i, 2)] = backward(0)
        for lo in range(2):
            forward = lax.dot_general(
                tok[q], block[lo], (((1,), (1,)), ((), ())), preferred_element_type=F32
            )

            @pl.when(i == 0)
            def _():
                out_acc[lo] = forward

            @pl.when(i > 0)
            def _():
                out_acc[lo] += forward

        @pl.when(i > 0)
        def _():
            close_ig(i - 1)

        after(i, 1, next_reduce(0))
        after(i, 2, combine(1))
        after(i, 3, next_reduce(1))
        after(i, 4, combine(2))
        after(i, 5, update)
        after(i, 6, copy_start)
        after(i, 7, copy_forward(0))
        return 0

    lax.fori_loop(0, N_CHUNK, against, 0)

    for lo in range(2):
        out_send[lo] = (out_acc[lo, pl.ds(TOK, TOK), :] * inv_width).astype(BF)
        push(out_send.at[lo], out_recv.at[lo], core_send.at[18 + lo], core_recv.at[18 + lo], sibling)
    copy_next()
    close_ig(N_CHUNK - 1)

    for lo in range(2):
        arrive(out_recv.at[lo], core_send.at[18 + lo], core_recv.at[18 + lo])
        own = (out_acc[lo, pl.ds(0, TOK), :] * inv_width).astype(BF)
        theirs = out_recv[lo]

        def write(low, high, lo=lo):
            base = lo * 896
            out_full[:, base:base + 384] = low[:, :384]
            out_full[:, base + 384:base + 512] = low[:, 384:] + high[:, :128]
            out_full[:, base + 512:base + 896] = high[:, 128:]

        @pl.when(c == 0)
        def _():
            write(own, theirs)

        @pl.when(c == 1)
        def _():
            write(theirs, own)

    store_outputs = pltpu.make_async_copy(out_full, outputs, load_sem.at[9])
    store_outputs.start()
    copy_forward(1)()
    for p in range(2):
        nc[p][1].finish()

    for k in range(3):
        store_state(k).wait()
    store_outputs.wait()
    for i in range(N_CHUNK):
        store_ig(i).wait()

    for p in range(3):
        for k in range(3):
            ag[p][k].close()
            rs[p][k].close()
    for p, (first, count, _) in enumerate(COPY_PARTS):
        left(copy_own.at[pl.ds(first, count)], nc_send.at[p], nc_recv.at[p])
        for k in range(2):
            nc[p][k].close()
    for lo in range(2):
        left(cot.at[lo, pl.ds(TOK, TOK)], core_send.at[lo], core_recv.at[lo])
        left(out_send.at[lo], core_send.at[18 + lo], core_recv.at[18 + lo])
    for i in range(N_CHUNK):
        left(tok.at[0, pl.ds(TOK, TOK)], core_send.at[2 + i], core_recv.at[2 + i])
        left(ig_send.at[i], core_send.at[10 + i], core_recv.at[10 + i])


def local(tokens, cotangent, master, moment_one, moment_two):
    vmem = pltpu.VMEM
    dma = pltpu.SemaphoreType.DMA
    hidden = cotangent.shape[1]
    width = tokens.shape[1]
    anywhere = pl.BlockSpec(memory_space=pl.ANY)
    state_shape = jax.ShapeDtypeStruct((ROWS, LANE), F32)
    got = []
    for stage in range(3):
        for p, (_, count, order) in enumerate(PARTS):
            if stage == 0:
                last = order[0]
                dims = tuple(2 if n == last else 4 for n in AXES if n != order[2])
                got.append(vmem((6,) + dims + (count, LANE), BF))
            elif stage == 1:
                got.append(vmem((6, 2, count, LANE), BF))
            else:
                got.append(vmem((6, count // 2, LANE), BF))
    results = pl.pallas_call(
        kernel,
        out_shape=(
            jax.ShapeDtypeStruct((TOK, hidden), BF),
            jax.ShapeDtypeStruct((TOK, width), BF),
            state_shape, state_shape, state_shape,
            jax.ShapeDtypeStruct((2, 4, 4, ROWS, LANE), BF),
        ),
        in_specs=[anywhere] * 5,
        out_specs=(anywhere,) * 6,
        scratch_shapes=[
            vmem((N_CHUNK, 2 * TOK, CHUNK), BF),
            vmem((2, 2 * TOK, PAD), BF),
            vmem((2, PAD, 2 * TOK), BF),
            vmem((4, 4, 4, PAD, LANE), BF),
            vmem((4, 4, 4, ROWS, LANE), BF),
            *got,
            vmem((ROWS, LANE), F32),
            vmem((2, 2 * TOK, PAD), F32),
            vmem((2, TOK, CHUNK), F32),
            vmem((N_CHUNK, TOK, CHUNK), BF),
            vmem((N_CHUNK, TOK, CHUNK), BF),
            vmem((2, TOK, PAD), BF),
            vmem((2, TOK, PAD), BF),
            vmem((TOK, hidden), BF),
            vmem((3, ROWS, LANE), F32),
            vmem((3, ROWS, LANE), F32),
            vmem((ROWS, LANE), BF),
            dma((10,)), dma((N_CHUNK,)), dma((N_CHUNK,)),
            dma((20,)), dma((20,)), dma((54,)), dma((54,)), dma((54,)), dma((54,)),
            dma((26,)), dma((26,)),
        ],
        compiler_params=pltpu.CompilerParams(
            collective_id=0, has_side_effects=True, vmem_limit_bytes=63 * 2**20
        ),
        name="step",
    )(tokens, cotangent, master, moment_one, moment_two)
    *rest, copies = results
    new_copy = copies.transpose(3, 0, 1, 2, 4).reshape(ROWS, width)
    return (*rest, new_copy)


def solution(mesh):
    placed = (
        P(("node", "dp"), None),
        P(("node", "dp"), None),
        P("node", "dp"),
        P("node", "dp"),
        P("node", "dp"),
    )
    return jax.shard_map(
        local,
        mesh=mesh,
        in_specs=placed,
        out_specs=(
            P(("node", "dp"), None),
            P(("node", "dp"), None),
            P("node", "dp"),
            P("node", "dp"),
            P("node", "dp"),
            P("node", None),
        ),
        check_vma=False,
    )
```

time: 711 us -> 144 us (0.20)
  waiting for transfers between devices: 642 us -> 0 us
  Pallas kernels: 0 us -> 121 us
  matrix products: 39.4 us -> 0 us
  between operations: 13.8 us -> 0.65 us
  local copies, waits for them, and re-layouts: 10.7 us -> 22.1 us
    all_gather x3 -> x0, waiting for transfers between devices: 315 us -> none  [the longest x2 183 us: spread_copy(): lax.all_gather(weights.astype(jnp.bfloat16), 'dp', axis=1, tiled=True)]
    unnamed x6 -> x0, waiting for transfers between devices: 194 us -> none
    reduce_scatter x1 -> x0, waiting for transfers between devices: 133 us -> none  [local(): lax.psum_scatter(lax.dot_general(cotangent, tokens, (((0,), (0,)), ((), (...]
    pallas_call x0 -> x1, Pallas kernels: none -> 121 us  [local(): pl.pallas_call(kernel, out_shape=(jax.ShapeDtypeStruct((TOK, hidden), BF)...]
    dot_general x3 -> x0, matrix products: 39.4 us -> none  [the longest x1 13.6 us: against_rows(): lax.dot_general(left, right, (((1,), (1,)), ((), ())), preferred_element_...]
    reshape x0 -> x1, local copies, waits for them, and re-layouts: none -> 7.28 us  [local(): new_copy = copies.transpose(3, 0, 1, 2, 4).reshape(ROWS, width)]
  transfers between devices with their start and end apart: 5 -> 0, of which waited for: 5 -> 0; matrix products, arithmetic and copies ran while one was open for 0% -> 0% of each run, Pallas kernels for 0% -> 0%
where the time goes in v1:
time: 144 us
  Pallas kernels  121 us (84%)
  local copies, waits for them, and re-layouts  22.1 us (15%)
    pallas_call x1, Pallas kernels, local(): pl.pallas_call(kernel, out_shape=(jax.ShapeDtypeStruct((TOK, hidden), BF)...  121 us
    unnamed x13, local copies, waits for them, and re-layouts  8.07 us
    reshape x1, local copies, waits for them, and re-layouts, local(): new_copy = copies.transpose(3, 0, 1, 2, 4).reshape(ROWS, width)  7.28 us
    transpose x1, local copies, waits for them, and re-layouts, local(): new_copy = copies.transpose(3, 0, 1, 2, 4).reshape(ROWS, width)  6.71 us

profile of v1, /device:TPU:0, one launch (start us, length us, event | category | flops | bytes accessed | tf_op | source)
XLA Modules:
  0.0 144.1 jit_solution(14885968503488883628)
XLA Ops:
  0.6 121.4 %step.1 = (bf16[512,1792]{1,0:T(8,128)(2,1)}, bf16[512,4096]{1,0:T(8,128)(2,1)}, f32[448,128]{1,0:T(8,128)}, f32[448,128]{1,0:T(8,128)}, f32[448,128]{1,0:T(8,128)}, /*index=5*/bf16[2,4,4,448,128]{4,3,2,1,0:T(8,128)(2,1)}) custom-call(bf16[512,4096]{1,0:T(8,128)(2,1)} %tokens.1, bf16[512,1792]{1,0:T(8,128)(2,1)} %cotangent.1, f32[448,128]{1,0:T(8,128)} %master.1, ...), custom_call_target="tpu_custom_call" | custom-call | tf_op jit(solution)/shard_map/step/pallas_call | solution.py:608
  122.0 6.7 %copy.11 = bf16[448,2,4,4,128]{4,3,2,1,0:T(4,128)(2,1)} copy(bf16[448,2,4,4,128]{4,0,3,2,1:T(8,128)(2,1)} %bitcast.1) | data formatting | bytes 7340032 | tf_op jit(solution)/shard_map/transpose | solution.py:646
  128.7 0.0 copy-start
  128.7 7.3 %reshape.15 = bf16[448,4096]{1,0:T(8,128)(2,1)} reshape(bf16[448,2,4,4,128]{4,3,2,1,0:T(4,128)(2,1)} %copy.11) | data formatting | bytes 7340032 | tf_op jit(solution)/shard_map/reshape | solution.py:646
  136.0 0.0 copy-done
  136.0 1.2 copy.17
  137.2 0.0 copy-start.3
  137.2 0.0 copy-start.2
  137.2 0.0 copy-start.1
  137.2 4.8 %copy.18 = bf16[512,4096]{1,0:T(8,128)(2,1)} copy(bf16[512,4096]{1,0:T(8,128)(2,1)} %get-tuple-element.25) | data formatting | bytes 8388608
  142.0 0.0 copy-done.3
  142.0 0.7 copy.19
  142.7 0.0 copy-done.2
  142.7 0.7 copy.20
  143.4 0.0 copy-done.1
  143.4 0.7 copy.21
Async XLA Ops:
  128.7 7.3 %copy-start = (bf16[512,1792]{1,0:T(8,128)(2,1)S(1)}, bf16[512,1792]{1,0:T(8,128)(2,1)}, u32[]{:S(2)}) copy-start(bf16[512,1792]{1,0:T(8,128)(2,1)} %get-tuple-element.24) | copy-start | bytes 5505028
  137.2 4.8 %copy-start.3 = (f32[448,128]{1,0:T(8,128)S(1)}, f32[448,128]{1,0:T(8,128)}, u32[]{:S(2)}) copy-start(f32[448,128]{1,0:T(8,128)} %get-tuple-element.26) | copy-start | bytes 688132
  137.2 5.5 %copy-start.2 = (f32[448,128]{1,0:T(8,128)S(1)}, f32[448,128]{1,0:T(8,128)}, u32[]{:S(2)}) copy-start(f32[448,128]{1,0:T(8,128)} %get-tuple-element.27) | copy-start | bytes 688132
  137.2 6.2 %copy-start.1 = (f32[448,128]{1,0:T(8,128)S(1)}, f32[448,128]{1,0:T(8,128)}, u32[]{:S(2)}) copy-start(f32[448,128]{1,0:T(8,128)} %get-tuple-element.28) | copy-start | bytes 688132

commit v2 on v0

v2 whole, which is shorter than its diff:
```python
import math

import jax
import jax.numpy as jnp
from jax import lax
from jax.experimental import pallas as pl
from jax.experimental.pallas import tpu as pltpu
from jax.sharding import PartitionSpec as P

beta_one = 0.9
beta_two = 0.95
epsilon = 1e-08
step_size = 0.2
decay_rate = 0.1
step_count = 10

MESH = pl.DeviceIdType.MESH
AXES = ("z", "x", "y")
BF = jnp.bfloat16
F32 = jnp.float32

ROWS = 448
PAD = 512
LANE = 128
TOK = 512
CHUNK = 512
N_CHUNK = 8
REDUCE_PARTS = ((0, 160, "zxy"), (160, 144, "xyz"), (304, 144, "yzx"))
GATHER_PARTS = (
    (0, 256, "z", "x", "y", ((0, 96, "y", "x"), (96, 160, "x", "y"))),
    (256, 96, "x", "z", "y", ((256, 96, "y", "z"),)),
    (352, 96, "y", "x", "z", ((352, 96, "z", "x"),)),
)
COPY_PARTS = ((0, 224, "xy"), (224, 224, "yx"))
REDUCE_TURNS = (2, 1, 3, 0)
GATHER_TURNS = (0, 1, 3, 2)
FAR = (1, 3, 2)


def device_at(co):
    return (
        lax.rem(co["z"], 2) * 2 + co["c"],
        lax.div(co["z"], 2) * 16 + co["x"] * 4 + co["y"],
    )


def moved(co, axis, by):
    other = dict(co)
    other[axis] = lax.rem(co[axis] + by + 4, 4)
    return other


def kernel(
    tokens, cotangent, master, moment_one, moment_two,
    out_full, ig_recv, state_new, copies,
    tok, cot, cot_t, weights, terms,
    got1a, got1b, got1c, got2a, got2b, got2c, got3a, got3b, got3c,
    grad_sum, out_acc, ig_own, ig_send, out_send, out_recv, state,
    load_sem, tok_sem,
    core_send, core_recv, ag_send, ag_recv, rs_send, rs_recv, nc_send, nc_recv,
):
    node = lax.axis_index("node")
    dp = lax.axis_index("dp")
    c = lax.rem(node, 2)
    z_lo = lax.div(node, 2)
    z_hi = lax.div(dp, 16)
    me = {
        "z": z_hi * 2 + z_lo,
        "x": lax.rem(lax.div(dp, 4), 4),
        "y": lax.rem(dp, 4),
        "c": c,
    }
    sibling = device_at({**me, "c": 1 - c})
    opposite_z = device_at(moved(me, "z", 2))
    window = [pl.multiple_of(lo * 896 + c * 384, 128) for lo in range(2)]
    sib_window = [pl.multiple_of(lo * 896 + (1 - c) * 384, 128) for lo in range(2)]
    offset = c * 64

    def remote(src, dst, send, recv, to):
        return pltpu.make_async_remote_copy(
            src_ref=src, dst_ref=dst, send_sem=send, recv_sem=recv,
            device_id=to, device_id_type=MESH,
        )

    def push(src, dst, send, recv, to):
        remote(src, dst, send, recv, to).start()

    def left(src, send, recv):
        remote(src, src, send, recv, sibling).wait_send()

    def arrive(dst, send, recv):
        remote(dst, dst, send, recv, sibling).wait_recv()

    def load_state(k):
        return pltpu.make_async_copy(
            (master, moment_one, moment_two)[k], state.at[k], load_sem.at[k]
        )

    def load_cot(lo):
        return pltpu.make_async_copy(
            cotangent.at[:, pl.ds(window[lo], PAD)],
            cot.at[lo, pl.ds(0, TOK)],
            load_sem.at[3 + lo],
        )

    def half_of(i):
        return lax.rem(z_hi + 1 + i, 2)

    def term_chunk(i):
        j = lax.div(i, 2)
        turn = 2 - j + lax.div(j, 2) * (3 - 2 * lax.rem(j, 2))
        return half_of(i), lax.rem(me["x"] + turn + 4, 4)

    def pass_chunk(i):
        j = lax.div(i, 2)
        turn = j + lax.div(j, 2) * (1 - 2 * lax.rem(j, 2))
        return half_of(i), lax.rem(me["x"] + turn, 4)

    def columns(q):
        return pl.ds(pl.multiple_of(q * CHUNK, CHUNK), CHUNK)

    def load_tok(i):
        hi, x = term_chunk(i)
        q = hi * 4 + x
        return pltpu.make_async_copy(
            tokens.at[:, columns(q)], tok.at[q, pl.ds(0, TOK)], tok_sem.at[i]
        )

    barrier = pltpu.get_barrier_semaphore()
    peers = [sibling]
    for axis in AXES:
        peers += [device_at(moved(me, axis, by)) for by in FAR]
    for peer in peers:
        pl.semaphore_signal(barrier, inc=1, device_id=peer, device_id_type=MESH)
    load_state(0).start()
    load_cot(0).start()
    load_cot(1).start()
    for i in range(N_CHUNK):
        load_tok(i).start()
    load_state(1).start()
    load_state(2).start()

    spare = pl.multiple_of((1 - c) * ROWS, 64)

    def clear(j, _):
        at = (lax.div(j, 16), lax.rem(lax.div(j, 4), 4), lax.rem(j, 4), pl.ds(spare, PAD - ROWS), slice(None))
        weights[at] = jnp.zeros((PAD - ROWS, LANE), BF)
        return 0

    lax.fori_loop(0, 64, clear, 0)
    pl.semaphore_wait(barrier, len(peers))

    def place(axis, by):
        return lax.rem(me[axis] + by + 4, 4)

    def pair(half):
        return pl.ds(2 * half, 2)

    every = slice(None)

    class Gather:
        def __init__(self, first, count, ring, turn_axis, half_axis, planes, base):
            self.first, self.count, self.ring = first, count, ring
            self.turn_axis, self.half_axis, self.planes = turn_axis, half_axis, planes
            self.base = base

        def at(self, spec, first, count):
            rows = pl.ds(pl.multiple_of(offset + first, 16), count)
            spec = {**{axis: me[axis] for axis in AXES}, **spec}
            return weights.at[spec["z"], spec["x"], spec["y"], rows, :]

        def sems(self, k):
            return ag_send.at[self.base + k], ag_recv.at[self.base + k]

        def first_start(self):
            for n, (first, count, one, two) in enumerate(self.planes):
                for by in FAR:
                    ref = self.at({}, first, count)
                    push(ref, ref, *self.sems(n * 6 + by - 1), device_at(moved(me, one, by)))

        def first_wait(self):
            for n, (first, count, one, two) in enumerate(self.planes):
                for by in FAR:
                    arrive(self.at({one: place(one, -by)}, first, count), *self.sems(n * 6 + by - 1))

        def second_start(self):
            for n, (first, count, one, two) in enumerate(self.planes):
                for by in FAR:
                    ref = self.at({one: every}, first, count)
                    push(ref, ref, *self.sems(n * 6 + 2 + by), device_at(moved(me, two, by)))

        def second_wait(self):
            for n, (first, count, one, two) in enumerate(self.planes):
                for by in FAR:
                    arrive(self.at({one: every, two: place(two, -by)}, first, count), *self.sems(n * 6 + 2 + by))

        def part(self, turn, half, where):
            spec = {
                self.turn_axis: place(self.turn_axis, GATHER_TURNS[turn]),
                self.half_axis: pair(half),
                self.ring: place(self.ring, where),
            }
            return self.at(spec, self.first, self.count)

        def ring_sems(self, turn, way, message):
            return self.sems(12 + turn * 6 + way * 3 + message)

        def start(self, turn):
            for message in range(2):
                for way in range(2):
                    ref = self.part(turn, message if way == 0 else 1 - message, 0)
                    push(ref, ref, *self.ring_sems(turn, way, message), device_at(moved(me, self.ring, 1 - 2 * way)))

        def forward(self, turn):
            for way in range(2):
                ref = self.part(turn, way, 2 * way - 1)
                arrive(ref, *self.ring_sems(turn, way, 0))
                push(ref, ref, *self.ring_sems(turn, way, 2), device_at(moved(me, self.ring, 1 - 2 * way)))

        def finish(self, turn):
            for way in range(2):
                arrive(self.part(turn, 1 - way, 2 * way - 1), *self.ring_sems(turn, way, 1))
                arrive(self.part(turn, way, 2), *self.ring_sems(turn, way, 2))

        def close(self):
            for n, (first, count, one, two) in enumerate(self.planes):
                for by in FAR:
                    left(self.at({}, first, count), *self.sems(n * 6 + by - 1))
                    left(self.at({one: every}, first, count), *self.sems(n * 6 + 2 + by))
            for turn in range(4):
                for k in range(6):
                    left(self.part(turn, 0, 0), *self.sems(12 + turn * 6 + k))

    ag = [Gather(*part, p * 36) for p, part in enumerate(GATHER_PARTS)]
    ag_z, ag_x, ag_y = ag

    class Copies:
        def __init__(self, order, first, count, z_half, base):
            self.one, self.two = order
            self.first, self.count, self.z_half, self.base = first, count, z_half, base

        def at(self, one, two, half=None):
            spec = {self.one: one, self.two: two}
            rows = pl.ds(self.first, self.count)
            if half is not None:
                rows = pl.ds(self.first + half * self.count // 2, self.count // 2)
            return copies.at[self.z_half, spec["x"], spec["y"], rows, :]

        def sems(self, k):
            return nc_send.at[self.base + k], nc_recv.at[self.base + k]

        def first_start(self):
            ref = self.at(me[self.one], me[self.two])
            for by in FAR:
                push(ref, ref, *self.sems(by - 1), device_at(moved(me, self.one, by)))

        def first_wait(self, by):
            arrive(self.at(place(self.one, -by), me[self.two]), *self.sems(by - 1))

        def part(self, by, half, where):
            return self.at(place(self.one, by), place(self.two, where), half)

        def ring_sems(self, by, way, message):
            return self.sems(3 + by * 6 + way * 3 + message)

        def start(self, by):
            for message in range(2):
                for way in range(2):
                    ref = self.part(by, message if way == 0 else 1 - message, 0)
                    push(ref, ref, *self.ring_sems(by, way, message), device_at(moved(me, self.two, 1 - 2 * way)))

        def forward(self, by):
            for way in range(2):
                ref = self.part(by, way, 2 * way - 1)
                arrive(ref, *self.ring_sems(by, way, 0))
                push(ref, ref, *self.ring_sems(by, way, 2), device_at(moved(me, self.two, 1 - 2 * way)))

        def finish(self, by):
            for way in range(2):
                arrive(self.part(by, 1 - way, 2 * way - 1), *self.ring_sems(by, way, 1))
                arrive(self.part(by, way, 2), *self.ring_sems(by, way, 2))

        def close(self):
            for by in FAR:
                left(self.at(me[self.one], me[self.two]), *self.sems(by - 1))
            for by in range(4):
                for k in range(6):
                    left(self.part(by, 0, 0), *self.sems(3 + by * 6 + k))

    nc = [
        [
            Copies(order, first, count, z_half, 2 + (g * 2 + p) * 27)
            for p, (first, count, order) in enumerate(COPY_PARTS)
        ]
        for g, z_half in enumerate((z_hi, 1 - z_hi))
    ]

    class Reduce:
        def __init__(self, order, first, count, got, base):
            self.one, self.two, self.three = order
            self.rows = pl.ds(first, count)
            self.got1, self.got2, self.got3 = got
            self.base = base

        def index(self, one, two, three):
            spec = {self.one: one, self.two: two, self.three: three}
            return spec["z"], spec["x"], spec["y"], self.rows, every

        def sems(self, k):
            return rs_send.at[self.base + k], rs_recv.at[self.base + k]

        def ring_index(self, turn, where, half):
            return self.index(place(self.one, where), place(self.two, REDUCE_TURNS[turn]), pair(half))

        def out(self, turn, where, half, slot, way):
            push(
                terms.at[self.ring_index(turn, where, half)], self.got1.at[turn, slot],
                *self.sems(turn * 6 + slot), device_at(moved(me, self.one, 1 - 2 * way)),
            )

        def far(self, turn):
            self.out(turn, 2, 0, 0, 0)
            self.out(turn, 2, 1, 1, 1)

        def near(self, turn, way):
            if way == 0:
                self.out(turn, 1, 1, 3, 0)
            else:
                self.out(turn, -1, 0, 5, 1)

        def combine(self, turn):
            for way in range(2):
                arrive(self.got1.at[turn, way], *self.sems(turn * 6 + way))
                at = self.ring_index(turn, 1 - 2 * way, way)
                total = terms[at].astype(F32) + self.got1[turn, way].astype(F32)
                terms[at] = total.astype(BF)
                self.out(turn, 1 - 2 * way, way, 2 if way == 0 else 4, way)

        def line(self, by):
            return self.index(me[self.one], place(self.two, by), every)

        def finish(self, turn):
            for half, (one, two) in enumerate(((2, 5), (3, 4))):
                arrive(self.got1.at[turn, one], *self.sems(turn * 6 + one))
                arrive(self.got1.at[turn, two], *self.sems(turn * 6 + two))
                at = self.ring_index(turn, 0, half)
                total = (
                    terms[at].astype(F32)
                    + self.got1[turn, one].astype(F32)
                    + self.got1[turn, two].astype(F32)
                )
                terms[at] = total.astype(BF)
            by = REDUCE_TURNS[turn]
            if by:
                push(
                    terms.at[self.line(by)], self.got2.at[by - 1],
                    *self.sems(23 + by), device_at(moved(me, self.two, by)),
                )

        def second(self):
            for by in FAR:
                arrive(self.got2.at[by - 1], *self.sems(23 + by))
            total = terms[self.line(0)].astype(F32)
            for k in range(3):
                total += self.got2[k].astype(F32)
            terms[self.line(0)] = total.astype(BF)
            for by in FAR:
                push(
                    terms.at[self.index(me[self.one], me[self.two], place(self.three, by))],
                    self.got3.at[by - 1], *self.sems(26 + by), device_at(moved(me, self.three, by)),
                )

        def third(self):
            for by in FAR:
                arrive(self.got3.at[by - 1], *self.sems(26 + by))
            total = terms[self.index(me[self.one], me[self.two], me[self.three])].astype(F32)
            for k in range(3):
                total += self.got3[k].astype(F32)
            grad_sum[self.rows, :] = total

        def close(self):
            for turn in range(4):
                for slot in range(6):
                    left(self.got1.at[turn, slot], *self.sems(turn * 6 + slot))
            for by in FAR:
                left(self.got2.at[by - 1], *self.sems(23 + by))
                left(self.got3.at[by - 1], *self.sems(26 + by))

    got = ((got1a, got2a, got3a), (got1b, got2b, got3b), (got1c, got2c, got3c))
    rs = [
        Reduce(order, first, count, got[p], p * 30)
        for p, (first, count, order) in enumerate(REDUCE_PARTS)
    ]
    rs_z, rs_x, rs_y = rs

    for lo in range(2):
        push(
            cotangent.at[:, pl.ds(sib_window[lo], PAD)], cot.at[lo, pl.ds(TOK, TOK)],
            core_send.at[lo], core_recv.at[lo], sibling,
        )
    for i in range(N_CHUNK):
        hi, x = term_chunk(i)
        q = hi * 4 + x
        push(
            tokens.at[:, columns(q)], tok.at[q, pl.ds(TOK, TOK)],
            core_send.at[2 + i], core_recv.at[2 + i], sibling,
        )

    load_state(0).wait()
    weights[me["z"], me["x"], me["y"], pl.ds(pl.multiple_of(offset, 32), ROWS), :] = state[0].astype(BF)
    for part in ag:
        part.first_start()
    for lo in range(2):
        load_cot(lo).wait()
        cot_t[lo, :, pl.ds(0, TOK)] = cot[lo, pl.ds(0, TOK), :].T
    for lo in range(2):
        arrive(cot.at[lo, pl.ds(TOK, TOK)], core_send.at[lo], core_recv.at[lo])
        cot_t[lo, :, pl.ds(TOK, TOK)] = cot[lo, pl.ds(TOK, TOK), :].T

    for part in ag:
        part.first_wait()
        part.second_start()

    def send_turn(parts, turn):
        for part in parts:
            part.far(turn)
            for way in range(2):
                part.near(turn, way)

    def term(i, _):
        hi, x = term_chunk(i)
        q = hi * 4 + x
        load_tok(i).wait()
        arrive(tok.at[q, pl.ds(TOK, TOK)], core_send.at[2 + i], core_recv.at[2 + i])
        for lo in range(2):
            part = jnp.dot(
                cot_t[lo, pl.ds(pl.multiple_of(offset, 64), ROWS), :], tok[q],
                preferred_element_type=F32,
            ).astype(BF)
            for y in range(4):
                terms[hi * 2 + lo, x, y] = part[:, y * LANE:(y + 1) * LANE]

        @pl.when(i == 1)
        def _():
            send_turn((rs_z,), 0)
            for turn in range(2):
                rs_x.far(turn)

        @pl.when(i == 3)
        def _():
            send_turn((rs_z,), 1)
            for turn in range(2):
                rs_x.near(turn, 0)

        @pl.when(i == 5)
        def _():
            for turn in range(2):
                rs_x.near(turn, 1)

        return 0

    lax.fori_loop(0, N_CHUNK, term, 0)

    def gather(action, *args):
        for part in ag:
            getattr(part, action)(*args)

    def reduce(action, *args):
        for part in rs:
            getattr(part, action)(*args)

    first = (rs_z, rs_x)

    def both(action, turn):
        for part in first:
            getattr(part, action)(turn)

    send_turn((rs_y,), 0)
    send_turn((rs_y,), 1)
    both("combine", 0)
    send_turn(first, 2)
    both("combine", 1)
    rs_y.combine(0)
    reduce("finish", 0)
    send_turn(rs, 3)
    send_turn((rs_y,), 2)
    rs_y.combine(1)
    both("combine", 2)
    reduce("finish", 1)
    gather("second_wait")
    rs_y.combine(2)
    both("combine", 3)
    reduce("finish", 2)
    rs_y.combine(3)
    gather("start", 0)
    ag_x.start(1)
    reduce("finish", 3)
    gather("forward", 0)
    ag_x.forward(1)
    reduce("second")
    ag_z.start(1)
    ag_x.start(2)
    ag_x.start(3)
    reduce("third")

    def update():
        load_state(1).wait()
        load_state(2).wait()
        grad = grad_sum[...] / math.sqrt(TOK * 128)
        one = beta_one * state[1] + (1.0 - beta_one) * grad
        two = beta_two * state[2] + (1.0 - beta_two) * grad * grad
        first_fix = 1.0 - beta_one**step_count
        second_fix = 1.0 - beta_two**step_count
        step = one / first_fix / (jnp.sqrt(two / second_fix) + epsilon)
        moved_master = state[0] - step_size * (step + decay_rate * state[0])
        state_new[0] = moved_master
        state_new[1] = one
        state_new[2] = two
        copies[z_hi, me["x"], me["y"]] = moved_master.astype(BF)
        for p, (first, count, _) in enumerate(COPY_PARTS):
            ref = copies.at[z_hi, me["x"], me["y"], pl.ds(first, count)]
            push(ref, ref, nc_send.at[p], nc_recv.at[p], opposite_z)
        for part in nc[0]:
            part.first_start()
            part.start(0)

    def copies_rest(g):
        def run():
            for by in FAR:
                for part in nc[g]:
                    part.first_wait(by)
                    part.start(4 - by)
        return run

    def copies_other():
        for p, (first, count, _) in enumerate(COPY_PARTS):
            arrive(
                copies.at[1 - z_hi, me["x"], me["y"], pl.ds(first, count)],
                nc_send.at[p], nc_recv.at[p],
            )
        for part in nc[1]:
            part.first_start()
            part.start(0)

    def copies_forward(g, *turns):
        def run():
            for by in turns:
                for part in nc[g]:
                    part.forward(by)
        return run

    def after_pass(step):
        if step == 0:
            copies_rest(0)()
            ag_x.forward(2)
            ag_x.forward(3)
            ag_z.forward(1)
            ag_y.forward(1)
        if step == 1:
            copies_other()
            ag_z.start(2)
            ag_y.start(2)
        if step == 2:
            copies_rest(1)()
            copies_forward(0, 0)()
            for turn in (1, 2, 3):
                ag_x.finish(turn)
            ag_z.finish(1)
            ag_y.finish(1)
        if step == 3:
            copies_forward(0, 3)()
            ag_z.forward(2)
            ag_y.forward(2)
        if step == 4:
            copies_forward(0, 1)()
            copies_forward(1, 0)()
            ag_z.start(3)
            ag_y.start(3)
        if step == 5:
            copies_forward(0, 2)()
            ag_z.finish(2)
            ag_y.finish(2)
        if step == 6:
            ag_z.forward(3)
            ag_y.forward(3)
            copies_forward(1, 3)()
        if step == 7:
            copies_forward(1, 1)()
        if step == 8:
            copies_forward(1, 2)()
            ag_z.finish(3)
            ag_y.finish(3)

    update()
    ag_y.start(1)
    gather("finish", 0)

    inv_width = 1.0 / math.sqrt(4096)
    inv_hidden = 1.0 / math.sqrt(1792)

    def ig_chunk(i):
        hi, x = pass_chunk(i)
        return hi * 4 + x

    def close_ig(i):
        q = ig_chunk(i)
        arrive(ig_recv.at[q], core_send.at[10 + i], core_recv.at[10 + i])
        total = ig_own[lax.rem(i, 2)] + ig_recv[q].astype(F32)
        ig_recv[q] = (total * inv_hidden).astype(BF)

    def against(j, _):
        chunks = [pass_chunk(2 * j + k) for k in range(2)]
        block = [
            [
                jnp.concatenate([weights[hi * 2 + lo, x, y] for y in range(4)], axis=1)
                for lo in range(2)
            ]
            for hi, x in chunks
        ]

        def events(k):
            for pair_at in range(4):
                if 3 * pair_at + k < 9:
                    pl.when(j == pair_at)(lambda step=3 * pair_at + k: after_pass(step))

        for k, (hi, x) in enumerate(chunks):
            q = hi * 4 + x
            i = 2 * j + k

            def backward(first):
                return sum(
                    jnp.dot(cot[lo, pl.ds(first, TOK), :], block[k][lo], preferred_element_type=F32)
                    for lo in range(2)
                )

            ig_send[i] = backward(TOK).astype(BF)
            push(ig_send.at[i], ig_recv.at[q], core_send.at[10 + i], core_recv.at[10 + i], sibling)
            ig_own[k] = backward(0)
            if k:
                close_ig(i - 1)
            else:

                @pl.when(j > 0)
                def _():
                    close_ig(i - 1)

            events(k)

        both = jnp.concatenate([tok[hi * 4 + x] for hi, x in chunks], axis=1)
        for lo in range(2):
            forward = lax.dot_general(
                both, jnp.concatenate([block[k][lo] for k in range(2)], axis=1),
                (((1,), (1,)), ((), ())), preferred_element_type=F32,
            )

            @pl.when(j == 0)
            def _():
                out_acc[lo] = forward

            @pl.when(j > 0)
            def _():
                out_acc[lo] += forward

        events(2)
        return 0

    lax.fori_loop(0, N_CHUNK // 2, against, 0)

    for lo in range(2):
        out_send[lo] = (out_acc[lo, pl.ds(TOK, TOK), :] * inv_width).astype(BF)
        push(out_send.at[lo], out_recv.at[lo], core_send.at[18 + lo], core_recv.at[18 + lo], sibling)
    close_ig(N_CHUNK - 1)

    for lo in range(2):
        arrive(out_recv.at[lo], core_send.at[18 + lo], core_recv.at[18 + lo])
        own = (out_acc[lo, pl.ds(0, TOK), :] * inv_width).astype(BF)
        theirs = out_recv[lo]

        def write(low, high, lo=lo):
            base = lo * 896
            out_full[:, base:base + 384] = low[:, :384]
            out_full[:, base + 384:base + 512] = low[:, 384:] + high[:, :128]
            out_full[:, base + 512:base + 896] = high[:, 128:]

        @pl.when(c == 0)
        def _():
            write(own, theirs)

        @pl.when(c == 1)
        def _():
            write(theirs, own)

    for g in range(2):
        for by in range(4):
            for part in nc[g]:
                part.finish(by)

    gather("close")
    reduce("close")
    for p, (first, count, _) in enumerate(COPY_PARTS):
        left(
            copies.at[z_hi, me["x"], me["y"], pl.ds(first, count)], nc_send.at[p], nc_recv.at[p]
        )
        for g in range(2):
            nc[g][p].close()
    for lo in range(2):
        left(cot.at[lo, pl.ds(TOK, TOK)], core_send.at[lo], core_recv.at[lo])
        left(out_send.at[lo], core_send.at[18 + lo], core_recv.at[18 + lo])
    for i in range(N_CHUNK):
        left(tok.at[0, pl.ds(TOK, TOK)], core_send.at[2 + i], core_recv.at[2 + i])
        left(ig_send.at[i], core_send.at[10 + i], core_recv.at[10 + i])


def local(tokens, cotangent, master, moment_one, moment_two):
    vmem = pltpu.VMEM
    dma = pltpu.SemaphoreType.DMA
    hidden = cotangent.shape[1]
    width = tokens.shape[1]
    anywhere = pl.BlockSpec(memory_space=pl.ANY)
    state_shape = jax.ShapeDtypeStruct((ROWS, LANE), F32)
    got = []
    for _, count, _ in REDUCE_PARTS:
        got.append(vmem((4, 6, 2, count, LANE), BF))
    for _, count, _ in REDUCE_PARTS:
        got.append(vmem((3, 4, count, LANE), BF))
    for _, count, _ in REDUCE_PARTS:
        got.append(vmem((3, count, LANE), BF))
    inside = pl.BlockSpec(memory_space=vmem)
    held = pl.pallas_call(
        kernel,
        out_shape=(
            vmem((TOK, hidden), BF),
            vmem((N_CHUNK, TOK, CHUNK), BF),
            vmem((3, ROWS, LANE), F32),
            vmem((2, 4, 4, ROWS, LANE), BF),
        ),
        in_specs=[anywhere] * 5,
        out_specs=(inside,) * 4,
        scratch_shapes=[
            vmem((N_CHUNK, 2 * TOK, CHUNK), BF),
            vmem((2, 2 * TOK, PAD), BF),
            vmem((2, PAD, 2 * TOK), BF),
            vmem((4, 4, 4, PAD, LANE), BF),
            vmem((4, 4, 4, ROWS, LANE), BF),
            *got,
            vmem((ROWS, LANE), F32),
            vmem((2, 2 * TOK, PAD), F32),
            vmem((2, TOK, CHUNK), F32),
            vmem((N_CHUNK, TOK, CHUNK), BF),
            vmem((2, TOK, PAD), BF),
            vmem((2, TOK, PAD), BF),
            vmem((3, ROWS, LANE), F32),
            dma((5,)), dma((N_CHUNK,)),
            dma((20,)), dma((20,)), dma((108,)), dma((108,)), dma((90,)), dma((90,)),
            dma((110,)), dma((110,)),
        ],
        compiler_params=pltpu.CompilerParams(
            collective_id=0, has_side_effects=True, vmem_limit_bytes=54 * 2**20
        ),
        name="step",
    )(tokens, cotangent, master, moment_one, moment_two)
    return pl.pallas_call(
        store,
        out_shape=(
            jax.ShapeDtypeStruct((TOK, hidden), BF),
            jax.ShapeDtypeStruct((TOK, width), BF),
            state_shape, state_shape, state_shape,
            jax.ShapeDtypeStruct((ROWS, width), BF),
        ),
        in_specs=[anywhere] * 4,
        out_specs=(anywhere,) * 6,
        scratch_shapes=[dma((44,))],
        compiler_params=pltpu.CompilerParams(has_side_effects=True, vmem_limit_bytes=2**20),
        name="store",
    )(*held)


def store(
    out_full, ig_full, state_new, copies,
    outputs, input_grad, new_master, new_one, new_two, new_copy, sem,
):
    moves = [(out_full, outputs)]
    for q in range(N_CHUNK):
        moves.append((ig_full.at[q], input_grad.at[:, pl.ds(q * CHUNK, CHUNK)]))
    for k, ref in enumerate((new_master, new_one, new_two)):
        moves.append((state_new.at[k], ref))
    for b in range(32):
        moves.append((
            copies.at[b // 16, (b // 4) % 4, b % 4], new_copy.at[:, pl.ds(b * LANE, LANE)],
        ))
    pending = [pltpu.make_async_copy(src, dst, sem.at[k]) for k, (src, dst) in enumerate(moves)]
    for copy in pending:
        copy.start()
    for copy in pending:
        copy.wait()


def solution(mesh):
    placed = (
        P(("node", "dp"), None),
        P(("node", "dp"), None),
        P("node", "dp"),
        P("node", "dp"),
        P("node", "dp"),
    )
    return jax.shard_map(
        local,
        mesh=mesh,
        in_specs=placed,
        out_specs=(
            P(("node", "dp"), None),
            P(("node", "dp"), None),
            P("node", "dp"),
            P("node", "dp"),
            P("node", "dp"),
            P("node", None),
        ),
        check_vma=False,
    )
```

time: 711 us -> 116 us (0.16)
  waiting for transfers between devices: 642 us -> 0 us
  Pallas kernels: 0 us -> 114 us
  matrix products: 39.4 us -> 0 us
  between operations: 13.8 us -> 0.64 us
  local copies, waits for them, and re-layouts: 10.7 us -> 0 us
    all_gather x3 -> x0, waiting for transfers between devices: 315 us -> none  [the longest x2 183 us: spread_copy(): lax.all_gather(weights.astype(jnp.bfloat16), 'dp', axis=1, tiled=True)]
    unnamed x6 -> x0, waiting for transfers between devices: 194 us -> none
    reduce_scatter x1 -> x0, waiting for transfers between devices: 133 us -> none  [local(): lax.psum_scatter(lax.dot_general(cotangent, tokens, (((0,), (0,)), ((), (...]
    pallas_call x0 -> x2, Pallas kernels: none -> 114 us  [the longest x1 110 us: local(): pl.pallas_call(kernel, out_shape=(vmem((TOK, hidden), BF), vmem((N_CHUNK,...]
    dot_general x3 -> x0, matrix products: 39.4 us -> none  [the longest x1 13.6 us: against_rows(): lax.dot_general(left, right, (((1,), (1,)), ((), ())), preferred_element_...]
    unnamed x15 -> x0, local copies, waits for them, and re-layouts: 10.7 us -> none
  transfers between devices with their start and end apart: 5 -> 0, of which waited for: 5 -> 0; matrix products, arithmetic and copies ran while one was open for 0% -> 0% of each run, Pallas kernels for 0% -> 0%
where the time goes in v2:
time: 116 us; the launch traced here: 115 us
  Pallas kernels  114 us (98%)
    pallas_call x1, Pallas kernels, local(): pl.pallas_call(kernel, out_shape=(vmem((TOK, hidden), BF), vmem((N_CHUNK,...  110 us
    pallas_call x1, Pallas kernels, local(): pl.pallas_call(store, out_shape=(jax.ShapeDtypeStruct((TOK, hidden), BF),...  4.25 us

profile of v2, /device:TPU:0, one launch (start us, length us, event | category | flops | bytes accessed | tf_op | source)
XLA Modules:
  0.0 114.7 jit_solution(16495894582590485070)
XLA Ops:
  0.6 109.8 %step.1 = (bf16[512,1792]{1,0:T(8,128)(2,1)S(1)}, bf16[8,512,512]{2,1,0:T(8,128)(2,1)S(1)}, f32[3,448,128]{2,1,0:T(8,128)S(1)}, bf16[2,4,4,448,128]{4,3,2,1,0:T(8,128)(2,1)S(1)}) custom-call(bf16[512,4096]{1,0:T(8,128)(2,1)} %tokens.1, bf16[512,1792]{1,0:T(8,128)(2,1)} %cotangent.1, f32[448,128]{1,0:T(8,128)} %master.1, f32[448,128]{1,0:T(8,128)} %moment_one.1, ...), custom_call_target="tpu_custom_call" | custom-call | tf_op jit(solution)/shard_map/step/pallas_call | solution.py:729
  110.4 4.2 %store.1 = (bf16[512,1792]{1,0:T(8,128)(2,1)}, bf16[512,4096]{1,0:T(8,128)(2,1)}, f32[448,128]{1,0:T(8,128)}, f32[448,128]{1,0:T(8,128)}, f32[448,128]{1,0:T(8,128)}, /*index=5*/bf16[448,4096]{1,0:T(8,128)(2,1)}) custom-call(bf16[512,1792]{1,0:T(8,128)(2,1)S(1)} %get-tuple-element.10.out_full, bf16[8,512,512]{2,1,0:T(8,128)(2,1)S(1)} %get-tuple-element.11.ig_full, ...), custom_call_target="tpu_custom_call" | custom-call | tf_op jit(solution)/shard_map/store/pallas_call | solution.py:762

commit v3 on v2

--- a/solution.py
+++ b/solution.py
@@ -148,6 +148,9 @@
         return 0
 
     lax.fori_loop(0, 64, clear, 0)
+    for lo in range(2):
+        load_cot(lo).wait()
+        cot_t[lo, :, pl.ds(0, TOK)] = cot[lo, pl.ds(0, TOK), :].T
     pl.semaphore_wait(barrier, len(peers))
 
     def place(axis, by):
@@ -410,9 +413,6 @@
     weights[me["z"], me["x"], me["y"], pl.ds(pl.multiple_of(offset, 32), ROWS), :] = state[0].astype(BF)
     for part in ag:
         part.first_start()
-    for lo in range(2):
-        load_cot(lo).wait()
-        cot_t[lo, :, pl.ds(0, TOK)] = cot[lo, pl.ds(0, TOK), :].T
     for lo in range(2):
         arrive(cot.at[lo, pl.ds(TOK, TOK)], core_send.at[lo], core_recv.at[lo])
         cot_t[lo, :, pl.ds(TOK, TOK)] = cot[lo, pl.ds(TOK, TOK), :].T
@@ -593,6 +593,7 @@
 
     update()
     ag_y.start(1)
+    reduce("close")
     gather("finish", 0)
 
     inv_width = 1.0 / math.sqrt(4096)
@@ -690,13 +691,12 @@
         def _():
             write(theirs, own)
 
+    gather("close")
     for g in range(2):
         for by in range(4):
             for part in nc[g]:
                 part.finish(by)
 
-    gather("close")
-    reduce("close")
     for p, (first, count, _) in enumerate(COPY_PARTS):
         left(
             copies.at[z_hi, me["x"], me["y"], pl.ds(first, count)], nc_send.at[p], nc_recv.at[p]

time: 116 us -> 116 us (level)
  no operation moved by 1% of the time
where the time goes in v3:
time: 116 us; the launch traced here: 114 us
  Pallas kernels  114 us (98%)
    pallas_call x1, Pallas kernels, local(): pl.pallas_call(kernel, out_shape=(vmem((TOK, hidden), BF), vmem((N_CHUNK,...  109 us
    pallas_call x1, Pallas kernels, local(): pl.pallas_call(store, out_shape=(jax.ShapeDtypeStruct((TOK, hidden), BF),...  4.25 us

profile of v3, /device:TPU:0, one launch (start us, length us, event | category | flops | bytes accessed | tf_op | source)
XLA Modules:
  0.0 114.3 jit_solution(1148391635703195436)
XLA Ops:
  0.6 109.4 %step.1 = (bf16[512,1792]{1,0:T(8,128)(2,1)S(1)}, bf16[8,512,512]{2,1,0:T(8,128)(2,1)S(1)}, f32[3,448,128]{2,1,0:T(8,128)S(1)}, bf16[2,4,4,448,128]{4,3,2,1,0:T(8,128)(2,1)S(1)}) custom-call(bf16[512,4096]{1,0:T(8,128)(2,1)} %tokens.1, bf16[512,1792]{1,0:T(8,128)(2,1)} %cotangent.1, f32[448,128]{1,0:T(8,128)} %master.1, f32[448,128]{1,0:T(8,128)} %moment_one.1, ...), custom_call_target="tpu_custom_call" | custom-call | tf_op jit(solution)/shard_map/step/pallas_call | solution.py:729
  110.1 4.2 %store.1 = (bf16[512,1792]{1,0:T(8,128)(2,1)}, bf16[512,4096]{1,0:T(8,128)(2,1)}, f32[448,128]{1,0:T(8,128)}, f32[448,128]{1,0:T(8,128)}, f32[448,128]{1,0:T(8,128)}, /*index=5*/bf16[448,4096]{1,0:T(8,128)(2,1)}) custom-call(bf16[512,1792]{1,0:T(8,128)(2,1)S(1)} %get-tuple-element.10.out_full, bf16[8,512,512]{2,1,0:T(8,128)(2,1)S(1)} %get-tuple-element.11.ig_full, ...), custom_call_target="tpu_custom_call" | custom-call | tf_op jit(solution)/shard_map/store/pallas_call | solution.py:762
